TPU v7x, 32 devices: a whole 2x2x4 slice. The times are simulated.
32 devices in a mesh: dp: 4 (over y, x), expert: 8 (over z, core).
Axes of the slice: x: 2, y: 2, z: 4, core: 2. Of those that a mesh axis runs over, the one named last changes fastest.
Arguments:
- activations: bfloat16 [1024, 7168], P('expert'), may hold values from -0.25 to 0.25
- expert_ids: int32 [1024, 8], P('expert'), may hold values from 0 to 31, all different within a row; in each aligned block of 128 rows (0 to 127, 128 to 255, ...) at most 48 rows name the same one
- gate_weights: float32 [1024, 8], P('expert'), may hold values from 0.2 to 1
- slot_grads: bfloat16 [32, 384, 1024], P('expert', 'dp'), may hold values from -6 to 6
- expert_weights: bfloat16 [32, 7168, 1024], P('expert', 'dp'), may hold values from -0.1875 to 0.1875
- shared_grads: bfloat16 [1024, 1024], P('expert'), may hold values from -6 to 6
- shared_weight: bfloat16 [7168, 1024], P('dp'), may hold values from -0.1875 to 0.1875
Outputs:
- rotation_grad: float32 [7168, 7168], P('expert', 'dp')
Inputs may be any that keep to these rules, and one draw needn't show every extreme that they name: `expert_ids`: each token names 8 different experts. In each aligned block of 128 tokens no expert is named by more than 48 tokens, a bound that some block reaches.
All inputs are finite; a program needn't handle non-finite values.
Results may differ from a plain program's by a relative error of at most 0.0075.
Values may be sent and summed in bfloat16 or wider, within the bound.
A program may use at most 192 MiB of HBM per device.

v0:
```python
import jax
import jax.numpy as jnp
from jax import lax
from jax.sharding import PartitionSpec as P


def slot_places(block_ids):
    flattened = block_ids.reshape(-1)
    positions = jnp.arange(flattened.shape[0], dtype=jnp.int32)
    matches = (flattened[:, None] == flattened[None, :]) & (positions[None, :] < positions[:, None])
    return jnp.sum(matches.astype(jnp.int32), axis=1).reshape(block_ids.shape)


def on_device(
    activations, expert_ids, gate_weights, slot_grads, expert_weights, shared_grads, shared_weight
):
    local_experts = expert_weights.shape[0]
    feature_block = expert_weights.shape[1]
    groups = lax.axis_size("expert")
    slot_total = slot_grads.shape[1] * lax.axis_size("dp")
    capacity = slot_total // groups
    partial_value = jnp.einsum(
        "esf,edf->esd",
        lax.all_gather(slot_grads, "dp", axis=1, tiled=True),
        expert_weights,
        preferred_element_type=jnp.float32,
    ).astype(jnp.bfloat16)
    partial_value = partial_value.reshape(local_experts, groups, capacity, feature_block)
    arrived = lax.all_to_all(partial_value, "expert", split_axis=1, concat_axis=0, tiled=True)
    arrived = arrived.reshape(local_experts * groups * capacity, feature_block)
    places = slot_places(expert_ids)
    row_index = expert_ids * capacity + places
    picked = jnp.take(arrived, row_index, axis=0).astype(jnp.float32)
    shared_term = jnp.einsum(
        "tf,df->td", shared_grads, shared_weight, preferred_element_type=jnp.float32
    )
    combined = (jnp.einsum("tk,tkd->td", gate_weights, picked) + shared_term).astype(jnp.bfloat16)
    columns = lax.all_to_all(activations, "expert", split_axis=1, concat_axis=0, tiled=True)
    return jnp.einsum(
        "tr,td->rd",
        columns,
        lax.all_gather(combined, "expert", axis=0, tiled=True),
        preferred_element_type=jnp.float32,
    )


def solution(mesh):
    return jax.shard_map(
        on_device,
        mesh=mesh,
        in_specs=(
            P("expert", None),
            P("expert", None),
            P("expert", None),
            P("expert", "dp", None),
            P("expert", "dp", None),
            P("expert", None),
            P("dp", None),
        ),
        out_specs=P("expert", "dp"),
        check_vma=False,
    )
```

profile of v0, /device:TPU:0, one launch (start us, length us, event | category | flops | bytes accessed | tf_op | source)
XLA Modules:
  0.0 327.2 jit_solution(11338813418159349779)
XLA Ops:
  6.5 0.0 copy-start
  6.5 0.0 all-gather.3.cloned.1.call-start
  6.5 0.7 all-gather.3.cloned.1.call-update
  7.3 48.7 %all-gather.3.cloned.1.call-done = bf16[4,384,1024]{2,1,0:T(8,128)(2,1)} async-done(((bf16[4,96,1024]{2,1,0:T(8,128)(2,1)}), bf16[4,384,1024]{2,1,0:T(8,128)(2,1)}) %all-gather.3.cloned.1.call-update) | async-done | bytes 3145744 | tf_op jit(solution)/shard_map/all_gather | solution.py:24
  55.9 17.1 %convolution_convert_fusion = bf16[4,384,1792]{2,1,0:T(8,128)(2,1)} fusion(bf16[4,384,1024]{2,1,0:T(8,128)(2,1)} %all-gather.3.cloned.1.call-done, bf16[4,1792,1024]{2,1,0:T(8,128)(2,1)} %param.11), kind=kOutput, calls=%fused_computation.1 | convolution fusion | flops 5639897088 | bytes 23330816 | tf_op jit(solution)/shard_map/esf,edf->esd/dot_general | solution.py:22
  73.0 5.5 %copy.40 = bf16[4,8,48,1792]{3,2,0,1:T(8,128)(2,1)} copy(bf16[4,8,48,1792]{3,2,1,0:T(8,128)(2,1)} %bitcast.26) | data formatting | bytes 11010048 | tf_op jit(solution)/shard_map/reshape | solution.py:28
  78.5 4.8 %all-to-all-start = ((bf16[4,8,48,1792]{3,2,0,1:T(8,128)(2,1)}), bf16[4,8,48,1792]{3,2,0,1:T(8,128)(2,1)}, u32[]{:S(2)}, u32[]{:S(2)}) async-start(bf16[4,8,48,1792]{3,2,0,1:T(8,128)(2,1)} %copy.40), calls=%async_computation | async-start | bytes 11010048 | tf_op jit(solution)/shard_map/all_to_all | solution.py:29
  83.4 0.0 all-gather.5.cloned.1.call-start
  83.4 0.0 copy-done.3
  83.4 0.1 copy.37
  83.5 0.1 eq.15
  83.6 0.5 convert_reduce_fusion
  84.1 0.1 reshape.20
  84.3 0.1 copy.41
  84.4 0.1 reshape.25
  84.5 0.1 copy.39
  84.6 0.0 copy-done.4
  84.6 0.1 copy.45
  84.8 120.7 %all-to-all-done = bf16[4,8,48,1792]{3,2,0,1:T(8,128)(2,1)} async-done(((bf16[4,8,48,1792]{3,2,0,1:T(8,128)(2,1)}), bf16[4,8,48,1792]{3,2,0,1:T(8,128)(2,1)}, u32[]{:S(2)}, u32[]{:S(2)}) %all-to-all-start) | async-done | bytes 5505056 | tf_op jit(solution)/shard_map/all_to_all | solution.py:29
  205.5 11.2 %gather_fusion = bf16[1024,1792]{1,0:T(8,128)(2,1)} fusion(bf16[1536,1792]{1,0:T(8,128)(2,1)} %bitcast.3, s32[1024]{0:T(1024)S(1)} %broadcast_clamp_fusion), kind=kCustom, calls=%fused_computation | custom fusion | bytes 7344128 | tf_op jit(solution)/shard_map/jit(_take)/gather | solution.py:33
  216.7 3.4 %fusion.1 = f32[128,1,1792]{2,1,0:T(1,128)S(1)} fusion(bf16[128,8,1]{1,2,0:T(2,128)(2,1)S(1)} %copy.45, bf16[1024,1792]{1,0:T(8,128)(2,1)} %gather_fusion, pred[128,8]{1,0:T(8,128)(4,1)S(1)} %copy.39), kind=kOutput, calls=%fused_computation.7 | convolution fusion | flops 5505024 | bytes 4590592 | tf_op jit(solution)/shard_map/tk,tkd->td/dot_general | solution.py:37
  220.1 0.0 copy-done
  220.1 0.0 copy-done.1
  220.1 0.0 copy-start.2
  220.1 2.1 fusion.3
  222.2 0.0 all-gather.5.cloned.1.call-update
  222.2 0.0 copy-done.2
  222.2 2.3 copy.42
  224.5 76.1 %all_to_all.34 = bf16[128,8,896]{0,2,1:T(8,128)(2,1)S(1)} all-to-all(bf16[128,8,896]{0,2,1:T(8,128)(2,1)} %bitcast.25), channel_id=1, replica_groups=mesh['dp'=4,'expert'=8] {'expert'}, dimensions={1} | all-to-all | bytes 3670016 | tf_op jit(solution)/shard_map/all_to_all | solution.py:38
  300.7 2.6 copy.43
  303.3 9.3 %convolution_bitcast_fusion = f32[896,1792]{0,1:T(8,128)} fusion(bf16[1024,1792]{1,0:T(8,128)(2,1)} %all-gather.5.cloned.1.call-done, bf16[1024,896]{1,0:T(8,128)(2,1)} %bitcast.27), kind=kOutput, calls=%fused_computation.5 | convolution fusion | flops 3288334336 | bytes 11927552 | tf_op jit(solution)/shard_map/tr,td->rd/dot_general | solution.py:39
  312.6 7.8 %copy.44 = f32[896,1792]{1,0:T(8,128)} copy(f32[896,1792]{0,1:T(8,128)} %convolution_bitcast_fusion) | data formatting | bytes 12845056 | tf_op jit(solution)/shard_map/tr,td->rd/dot_general | solution.py:39
  (7 shorter events, 0.1 us)
Async XLA Ops:
  6.5 213.5 %copy-start = (bf16[128,1024]{1,0:T(8,128)(2,1)S(1)}, bf16[128,1024]{1,0:T(8,128)(2,1)}, u32[]{:S(2)}) copy-start(bf16[128,1024]{1,0:T(8,128)(2,1)} %param.12) | copy-start | bytes 786436
  6.5 49.4 %all-gather.3.cloned.1.call-start = ((), (), s32[]{:S(2)}) async-start(), calls=%async_computation.2 | async-start | bytes 3932160 | tf_op jit(solution)/shard_map/all_gather | solution.py:24
  78.5 4.9 %copy-start.3 = (s32[128,8]{0,1:T(8,128)S(1)}, s32[128,8]{0,1:T(8,128)}, u32[]{:S(2)}) copy-start(s32[128,8]{0,1:T(8,128)} %param.8) | copy-start | bytes 12292
  78.5 6.1 %copy-start.4 = (f32[128,8]{0,1:T(8,128)S(1)}, f32[128,8]{0,1:T(8,128)}, u32[]{:S(2)}) copy-start(f32[128,8]{0,1:T(8,128)} %param.9) | copy-start | bytes 12292
  78.5 126.9 %all-to-all-start = ((bf16[4,8,48,1792]{3,2,0,1:T(8,128)(2,1)}), bf16[4,8,48,1792]{3,2,0,1:T(8,128)(2,1)}, u32[]{:S(2)}, u32[]{:S(2)}) async-start(bf16[4,8,48,1792]{3,2,0,1:T(8,128)(2,1)} %copy.40), calls=%async_computation | async-start | bytes 11010048 | tf_op jit(solution)/shard_map/all_to_all | solution.py:29
  83.4 219.9 %all-gather.5.cloned.1.call-start = ((), (), s32[]{:S(2)}) async-start(), calls=%async_computation.3 | async-start | bytes 4128768 | tf_op jit(solution)/shard_map/all_gather | solution.py:42
  216.7 3.4 %copy-start.1 = (bf16[1792,1024]{1,0:T(8,128)(2,1)S(1)}, bf16[1792,1024]{1,0:T(8,128)(2,1)}, u32[]{:S(2)}) copy-start(bf16[1792,1024]{1,0:T(8,128)(2,1)} %param.13) | copy-start | bytes 11010052
  220.1 2.1 copy-start.2
Sparse Core Ops, SparseCore 0:
  9.2 46.6 all-gather.2
  222.3 74.8 all-gather.4
where the time goes:
time: 328 us; the launch traced here: 327 us
  waiting for transfers between devices  170 us (52%)
  blocking collectives  76.1 us (23%)
  matrix products  31.9 us (10%)
  local copies, waits for them, and re-layouts  30.2 us (9%)
  between operations  13.5 us (4%)
  starting transfers between devices  4.86 us (1%)
    all_to_all x1, waiting for transfers between devices, on_device(): lax.all_to_all(partial_value, 'expert', split_axis=1, concat_axis=0, tile...  121 us
    all_to_all x1, blocking collectives, on_device(): lax.all_to_all(activations, 'expert', split_axis=1, concat_axis=0, tiled=...  76.1 us
    all_gather x1, waiting for transfers between devices, on_device(): lax.all_gather(slot_grads, 'dp', axis=1, tiled=True)  48.7 us
    dot_general x1, matrix products, on_device(): jnp.einsum('esf,edf->esd', lax.all_gather(slot_grads, 'dp', axis=1, tiled...  17.1 us
    gather x1, local copies, waits for them, and re-layouts, on_device(): picked = jnp.take(arrived, row_index, axis=0).astype(jnp.float32)  11.2 us
    dot_general x1, matrix products, on_device(): jnp.einsum('tr,td->rd', columns, lax.all_gather(combined, 'expert', axis=...  9.33 us
    dot_general x1, local copies, waits for them, and re-layouts, on_device(): jnp.einsum('tr,td->rd', columns, lax.all_gather(combined, 'expert', axis=...  7.76 us
  transfers between devices with their start and end apart: 3, of which 2 were waited for; matrix products, arithmetic and copies ran while one was open for 2% of the time, Pallas kernels for 0%

commit v1 on v0

v1 whole, which is shorter than its diff:
```python
import jax
import jax.numpy as jnp
from jax import lax
from jax.sharding import PartitionSpec as P


def source_matrix(ids, gates, first, local_experts, groups, capacity):
    tokens = ids.shape[0]
    block = tokens // groups
    experts = first + jnp.arange(local_experts, dtype=jnp.int32)
    hit = ids[:, :, None] == experts[None, None, :]
    gate = jnp.sum(jnp.where(hit, gates[:, :, None], 0.0), axis=1)
    named = jnp.any(hit, axis=1)
    ones = named.astype(jnp.bfloat16).reshape(groups, block, local_experts)
    row = jnp.arange(block, dtype=jnp.int32)
    earlier = (row[None, :] < row[:, None]).astype(jnp.bfloat16)
    place = jnp.einsum("tu,bue->bte", earlier, ones, preferred_element_type=jnp.float32)
    place = place.astype(jnp.int32).reshape(tokens, local_experts)
    source = (jnp.arange(tokens, dtype=jnp.int32) // block)[:, None]
    slot = jnp.where(named, source * capacity + place, -1)
    slots = jnp.arange(groups * capacity, dtype=jnp.int32)
    spread = jnp.where(slot[:, :, None] == slots[None, None, :], gate[:, :, None], 0.0)
    return spread.astype(jnp.bfloat16).reshape(tokens, local_experts * groups * capacity)


def on_device(
    activations, expert_ids, gate_weights, slot_grads, expert_weights, shared_grads, shared_weight
):
    local_experts, feature_block = expert_weights.shape[:2]
    groups = lax.axis_size("expert")
    slot_total = slot_grads.shape[1] * lax.axis_size("dp")
    capacity = slot_total // groups
    block, width = activations.shape
    rows = width // groups

    ids = lax.all_gather(expert_ids, "expert", axis=0, tiled=True)
    gates = lax.all_gather(gate_weights, "expert", axis=0, tiled=True)
    gathered = lax.all_gather(slot_grads, "dp", axis=1, tiled=True)
    turned = activations.T.reshape(groups, rows, block)
    columns = lax.all_to_all(turned, "expert", split_axis=0, concat_axis=0, tiled=True)
    gathered, columns, ids, gates = lax.optimization_barrier((gathered, columns, ids, gates))
    columns = columns.transpose(1, 0, 2).reshape(rows, groups * block)

    partial_value = jnp.einsum(
        "esf,edf->esd", gathered, expert_weights, preferred_element_type=jnp.float32
    ).astype(jnp.bfloat16)
    partial_value = partial_value.reshape(local_experts * slot_total, feature_block)
    first = lax.axis_index("expert") * local_experts
    spread = source_matrix(ids, gates, first, local_experts, groups, capacity)
    own = jnp.dot(spread, partial_value, preferred_element_type=jnp.float32).astype(jnp.bfloat16)
    summed = lax.psum_scatter(own, "expert", scatter_dimension=0, tiled=True)
    shared_term = jnp.einsum(
        "tf,df->td", shared_grads, shared_weight, preferred_element_type=jnp.float32
    )
    combined = (summed.astype(jnp.float32) + shared_term).astype(jnp.bfloat16)
    combined = lax.all_gather(combined, "expert", axis=0, tiled=True)
    columns, combined = lax.optimization_barrier((columns, combined))
    return jnp.dot(columns, combined, preferred_element_type=jnp.float32)


def solution(mesh):
    return jax.shard_map(
        on_device,
        mesh=mesh,
        in_specs=(
            P("expert", None),
            P("expert", None),
            P("expert", None),
            P("expert", "dp", None),
            P("expert", "dp", None),
            P("expert", None),
            P("dp", None),
        ),
        out_specs=P("expert", "dp"),
        check_vma=False,
    )
```

time: 328 us -> 216 us (0.66)
  waiting for transfers between devices: 170 us -> 84.4 us
  local copies, waits for them, and re-layouts: 30.2 us -> 6.53 us
  blocking collectives: 76.1 us -> 63.5 us
  matrix products: 31.9 us -> 40.8 us
    all_to_all x1, waiting for transfers between devices: 121 us -> 0.01 us  [on_device(): lax.all_to_all(turned, 'expert', split_axis=0, concat_axis=0, tiled=True)]
    all_to_all x1 -> x0, blocking collectives: 76.1 us -> none  [on_device(): lax.all_to_all(activations, 'expert', split_axis=1, concat_axis=0, tiled=...]
    all_gather x0 -> x2, blocking collectives: none -> 63.5 us  [the longest x1 49.5 us: on_device(): ids = lax.all_gather(expert_ids, 'expert', axis=0, tiled=True)]
    reduce_scatter x0 -> x1, waiting for transfers between devices: none -> 45.2 us  [on_device(): summed = lax.psum_scatter(own, 'expert', scatter_dimension=0, tiled=True)]
    gather x1 -> x0, local copies, waits for them, and re-layouts: 11.2 us -> none  [on_device(): picked = jnp.take(arrived, row_index, axis=0).astype(jnp.float32)]
    all_gather x2, waiting for transfers between devices: 48.7 us -> 38.5 us  [the longest x1 38.5 us: on_device(): combined = lax.all_gather(combined, 'expert', axis=0, tiled=True)]
    dot_general x1 -> x0, local copies, waits for them, and re-layouts: 7.76 us -> none  [on_device(): jnp.einsum('tr,td->rd', columns, lax.all_gather(combined, 'expert', axis=...]
    dot_general x3 -> x4, matrix products: 29.8 us -> 36.6 us  [the longest x1 17.1 us: on_device(): jnp.einsum('esf,edf->esd', gathered, expert_weights, preferred_element_ty...]
  transfers between devices with their start and end apart: 3 -> 4, of which waited for: 2 -> 2; matrix products, arithmetic and copies ran while one was open for 2% -> 3% of each run, Pallas kernels for 0% -> 0%
where the time goes in v1:
time: 216 us; the launch traced here: 215 us
  waiting for transfers between devices  84.4 us (39%)
  blocking collectives  63.5 us (29%)
  matrix products  40.8 us (19%)
  between operations  13.2 us (6%)
  starting transfers between devices  6.59 us (3%)
  local copies, waits for them, and re-layouts  6.53 us (3%)
    all_gather x1, blocking collectives, on_device(): ids = lax.all_gather(expert_ids, 'expert', axis=0, tiled=True)  49.5 us
    reduce_scatter x1, waiting for transfers between devices, on_device(): summed = lax.psum_scatter(own, 'expert', scatter_dimension=0, tiled=True)  45.2 us
    all_gather x1, waiting for transfers between devices, on_device(): combined = lax.all_gather(combined, 'expert', axis=0, tiled=True)  38.5 us
    dot_general x1, matrix products, on_device(): jnp.einsum('esf,edf->esd', gathered, expert_weights, preferred_element_ty...  17.1 us
    all_gather x1, blocking collectives, on_device(): gates = lax.all_gather(gate_weights, 'expert', axis=0, tiled=True)  14 us
    dot_general x1, matrix products, on_device(): jnp.dot(spread, partial_value, preferred_element_type=jnp.float32)  10.4 us
    dot_general x1, matrix products, on_device(): return jnp.dot(columns, combined, preferred_element_type=jnp.float32)  8.88 us
    all_to_all x1, starting transfers between devices, on_device(): lax.all_to_all(turned, 'expert', split_axis=0, concat_axis=0, tiled=True)  6.33 us
  transfers between devices with their start and end apart: 4, of which 2 were waited for; matrix products, arithmetic and copies ran while one was open for 3% of the time, Pallas kernels for 0%

profile of v1, /device:TPU:0, one launch (start us, length us, event | category | flops | bytes accessed | tf_op | source)
XLA Modules:
  0.0 215.2 jit_solution(11404970722814509077)
XLA Ops:
  6.5 0.0 copy-start
  6.5 0.0 all-gather.3.cloned.1.call-start
  6.5 0.7 all-gather.3.cloned.1.call-update
  7.3 0.0 copy-start.1
  7.3 0.0 copy-start.2
  7.3 3.9 %copy.16 = bf16[128,7168]{0,1:T(8,128)(2,1)} copy(bf16[128,7168]{1,0:T(8,128)(2,1)} %param.7) | data formatting | bytes 3670016 | tf_op args[0]
  11.2 6.3 %all-to-all-start = ((bf16[8,896,128]{2,1,0:T(8,128)(2,1)}), bf16[8,896,128]{2,1,0:T(8,128)(2,1)S(1)}, u32[]{:S(2)}, u32[]{:S(2)}) async-start(bf16[8,896,128]{2,1,0:T(8,128)(2,1)} %bitcast.43), calls=%async_computation | async-start | bytes 3670016 | tf_op jit(solution)/shard_map/all_to_all | solution.py:40
  17.5 0.0 reduce-scatter.2.cloned.1.call-start
  17.5 0.0 copy-done.1
  17.5 49.5 %all_gather.13 = s32[1024,8]{0,1:T(8,128)S(1)} all-gather(s32[128,8]{0,1:T(8,128)S(1)} %copy-done.1), channel_id=1, replica_groups=mesh['dp'=4,'expert'=8] {'expert'}, dimensions={0}, use_global_device_ids=true | all-gather | bytes 36864 | tf_op jit(solution)/shard_map/all_gather | solution.py:36
  67.0 0.0 copy-done.2
  67.0 14.0 %all_gather.14 = f32[1024,8]{0,1:T(8,128)S(1)} all-gather(f32[128,8]{0,1:T(8,128)S(1)} %copy-done.2), channel_id=1, replica_groups=mesh['dp'=4,'expert'=8] {'expert'}, dimensions={0}, use_global_device_ids=true | all-gather | bytes 36864 | tf_op jit(solution)/shard_map/all_gather | solution.py:37
  81.0 0.0 all-to-all-done
  81.0 0.0 all-gather.3.cloned.1.call-done
  81.1 0.1 compare_reduce_fusion
  81.2 0.1 fusion.11
  81.3 0.1 fusion.10
  81.5 17.1 %fusion.40 = bf16[4,384,1792]{2,1,0:T(8,128)(2,1)} fusion(bf16[4,384,1024]{2,1,0:T(8,128)(2,1)} %all-gather.3.cloned.1.call-done, bf16[4,1792,1024]{2,1,0:T(8,128)(2,1)} %param.11), kind=kOutput, calls=%fused_computation.4.clone.clone.clone.2 | convolution fusion | flops 5639897088 | bytes 23330816 | tf_op jit(solution)/shard_map/esf,edf->esd/dot_general | solution.py:44
  98.6 10.4 %bitcast_convert_fusion = bf16[1024,1792]{1,0:T(8,128)(2,1)} fusion(bf16[1024,4]{0,1:T(4,128)(2,1)S(1)} %fusion.11, s32[1024,4]{0,1:T(4,128)S(1)} %fusion.14, bf16[4,384,1792]{2,1,0:T(8,128)(2,1)} %fusion.40), kind=kOutput, calls=%fused_computation | convolution fusion | flops 5642125312 | bytes 9199616 | tf_op jit(solution)/shard_map/dot_general | solution.py:50
  109.0 0.0 reduce-scatter.2.cloned.1.call-update
  109.0 0.2 all-gather.5.cloned.1.call-start
  109.3 45.2 %reduce-scatter.2.cloned.1.call-done = bf16[128,1792]{1,0:T(8,128)(2,1)} async-done(((bf16[1024,1792]{1,0:T(8,128)(2,1)}), bf16[128,1792]{1,0:T(8,128)(2,1)}) %reduce-scatter.2.cloned.1.call-update) | async-done | bytes 458768 | tf_op jit(solution)/shard_map/reduce_scatter | solution.py:51
  154.4 0.0 copy-done
  154.4 4.2 %fusion.9 = bf16[128,1792]{1,0:T(8,128)(2,1)} fusion(bf16[128,1024]{1,0:T(8,128)(2,1)S(1)} %copy-done, bf16[1792,1024]{1,0:T(8,128)(2,1)} %param.13, bf16[128,1792]{1,0:T(8,128)(2,1)} %reduce-scatter.2.cloned.1.call-done), kind=kOutput, calls=%fused_computation.10 | convolution fusion | flops 470450176 | bytes 4849664 | tf_op jit(solution)/shard_map/tf,df->td/dot_general | solution.py:52
  158.7 0.0 all-gather.5.cloned.1.call-update
  158.7 2.6 %copy.17 = bf16[896,8,128]{0,2,1:T(8,128)(2,1)} copy(bf16[896,8,128]{2,0,1:T(8,128)(2,1)S(1)} %bitcast.42) | data formatting | bytes 3670016 | tf_op jit(solution)/shard_map/transpose | solution.py:42
  161.3 38.5 %all-gather.5.cloned.1.call-done = bf16[1024,1792]{1,0:T(8,128)(2,1)} async-done(((bf16[128,1792]{1,0:T(8,128)(2,1)}), bf16[1024,1792]{1,0:T(8,128)(2,1)}) %all-gather.5.cloned.1.call-update) | async-done | bytes 3670032 | tf_op jit(solution)/shard_map/all_gather | solution.py:56
  199.8 8.9 %fusion.22 = f32[896,1792]{1,0:T(8,128)} fusion(bf16[896,1024]{0,1:T(8,128)(2,1)} %bitcast.44, bf16[1024,1792]{1,0:T(8,128)(2,1)} %all-gather.5.cloned.1.call-done), kind=kOutput, calls=%fused_computation.32 | convolution fusion | flops 3288334336 | bytes 11927552 | tf_op jit(solution)/shard_map/dot_general | solution.py:58
  (3 shorter events, 0.0 us)
Async XLA Ops:
  6.5 147.9 %copy-start = (bf16[128,1024]{1,0:T(8,128)(2,1)S(1)}, bf16[128,1024]{1,0:T(8,128)(2,1)}, u32[]{:S(2)}) copy-start(bf16[128,1024]{1,0:T(8,128)(2,1)} %param.12) | copy-start | bytes 786436
  6.5 74.5 %all-gather.3.cloned.1.call-start = ((), (), s32[]{:S(2)}) async-start(), calls=%async_computation.2 | async-start | bytes 3932160 | tf_op jit(solution)/shard_map/all_gather | solution.py:38
  7.3 10.3 %copy-start.1 = (s32[128,8]{0,1:T(8,128)S(1)}, s32[128,8]{0,1:T(8,128)}, u32[]{:S(2)}) copy-start(s32[128,8]{0,1:T(8,128)} %param.8) | copy-start | bytes 12292
  7.3 59.8 %copy-start.2 = (f32[128,8]{0,1:T(8,128)S(1)}, f32[128,8]{0,1:T(8,128)}, u32[]{:S(2)}) copy-start(f32[128,8]{0,1:T(8,128)} %param.9) | copy-start | bytes 12292
  11.2 69.9 %all-to-all-start = ((bf16[8,896,128]{2,1,0:T(8,128)(2,1)}), bf16[8,896,128]{2,1,0:T(8,128)(2,1)S(1)}, u32[]{:S(2)}, u32[]{:S(2)}) async-start(bf16[8,896,128]{2,1,0:T(8,128)(2,1)} %bitcast.43), calls=%async_computation | async-start | bytes 3670016 | tf_op jit(solution)/shard_map/all_to_all | solution.py:40
  17.5 137.0 %reduce-scatter.2.cloned.1.call-start = ((), (), s32[]{:S(2)}) async-start(), calls=%async_computation.3 | async-start | bytes 4128768 | tf_op jit(solution)/shard_map/reduce_scatter | solution.py:51
  109.0 90.8 %all-gather.5.cloned.1.call-start = ((), (), s32[]{:S(2)}) async-start(), calls=%async_computation.4 | async-start | bytes 4128768 | tf_op jit(solution)/shard_map/all_gather | solution.py:56
Sparse Core Ops, SparseCore 0:
  9.2 46.6 all-gather.2
  109.2 45.2 reduce-scatter.1
  158.8 40.9 all-gather.4

commit v2 on v1

--- a/solution.py
+++ b/solution.py
@@ -33,25 +33,38 @@
     block, width = activations.shape
     rows = width // groups
 
-    ids = lax.all_gather(expert_ids, "expert", axis=0, tiled=True)
-    gates = lax.all_gather(gate_weights, "expert", axis=0, tiled=True)
     gathered = lax.all_gather(slot_grads, "dp", axis=1, tiled=True)
+    routed = jnp.concatenate([expert_ids.astype(jnp.float32), gate_weights], axis=1)
+    routed = lax.all_gather(routed, "expert", axis=0, tiled=True)
     turned = activations.T.reshape(groups, rows, block)
+    turned, routed = lax.optimization_barrier((turned, routed))
     columns = lax.all_to_all(turned, "expert", split_axis=0, concat_axis=0, tiled=True)
-    gathered, columns, ids, gates = lax.optimization_barrier((gathered, columns, ids, gates))
-    columns = columns.transpose(1, 0, 2).reshape(rows, groups * block)
 
-    partial_value = jnp.einsum(
-        "esf,edf->esd", gathered, expert_weights, preferred_element_type=jnp.float32
-    ).astype(jnp.bfloat16)
-    partial_value = partial_value.reshape(local_experts * slot_total, feature_block)
+    top = expert_ids.shape[1]
+    ids, gates = routed[:, :top].astype(jnp.int32), routed[:, top:]
     first = lax.axis_index("expert") * local_experts
     spread = source_matrix(ids, gates, first, local_experts, groups, capacity)
-    own = jnp.dot(spread, partial_value, preferred_element_type=jnp.float32).astype(jnp.bfloat16)
-    summed = lax.psum_scatter(own, "expert", scatter_dimension=0, tiled=True)
     shared_term = jnp.einsum(
         "tf,df->td", shared_grads, shared_weight, preferred_element_type=jnp.float32
     )
+    gathered, spread, shared_term = lax.optimization_barrier((gathered, spread, shared_term))
+
+    parts = 2 if feature_block % 256 == 0 else 1
+    step = feature_block // parts
+    sums = []
+    for part in range(parts):
+        weights = expert_weights[:, part * step : (part + 1) * step]
+        partial_value = jnp.einsum(
+            "esf,edf->esd", gathered, weights, preferred_element_type=jnp.float32
+        ).astype(jnp.bfloat16)
+        partial_value = partial_value.reshape(local_experts * slot_total, step)
+        own = jnp.dot(spread, partial_value, preferred_element_type=jnp.float32)
+        own = own.astype(jnp.bfloat16)
+        if part == 0:
+            own, columns = lax.optimization_barrier((own, columns))
+        sums.append(lax.psum_scatter(own, "expert", scatter_dimension=0, tiled=True))
+    columns = columns.transpose(1, 0, 2).reshape(rows, groups * block)
+    summed = jnp.concatenate(sums, axis=1)
     combined = (summed.astype(jnp.float32) + shared_term).astype(jnp.bfloat16)
     combined = lax.all_gather(combined, "expert", axis=0, tiled=True)
     columns, combined = lax.optimization_barrier((columns, combined))

time: 216 us -> 203 us (0.940)
  blocking collectives: 63.5 us -> 15.6 us
  waiting for transfers between devices: 84.4 us -> 108 us
  local copies, waits for them, and re-layouts: 6.53 us -> 15.5 us
  other arithmetic: 0.27 us -> 7.66 us
  matrix products: 40.8 us -> 37 us
    all_gather x2 -> x1, blocking collectives: 63.5 us -> 15.6 us  [on_device(): routed = lax.all_gather(routed, 'expert', axis=0, tiled=True)]
    reduce_scatter x1 -> x2, waiting for transfers between devices: 45.2 us -> 57.2 us  [on_device(): lax.psum_scatter(own, 'expert', scatter_dimension=0, tiled=True)]
    convert_element_type x0 -> x4, other arithmetic: none -> 7.39 us  [the longest x1 5.48 us: source_matrix(): spread.astype(jnp.bfloat16)]
    all_to_all x1, waiting for transfers between devices: 0.01 us -> 7.07 us  [on_device(): lax.all_to_all(turned, 'expert', split_axis=0, concat_axis=0, tiled=True)]
    all_gather x1, waiting for transfers between devices: 0.02 us -> 5.52 us  [on_device(): gathered = lax.all_gather(slot_grads, 'dp', axis=1, tiled=True)]
    unnamed x7 -> x17, local copies, waits for them, and re-layouts: 3.89 us -> 7.69 us
    dot_general x2 -> x4, matrix products: 27.6 us -> 24.2 us  [the longest x2 15.1 us: on_device(): jnp.einsum('esf,edf->esd', gathered, weights, preferred_element_type=jnp....]
    broadcast_in_dim x0 -> x1, local copies, waits for them, and re-layouts: none -> 2.97 us  [source_matrix(): jnp.where(slot[:, :, None] == slots[None, None, :], gate[:, :, None], 0.0)]
  transfers between devices with their start and end apart: 4 -> 5, of which waited for: 2 -> 5; matrix products, arithmetic and copies ran while one was open for 3% -> 25% of each run, Pallas kernels for 0% -> 0%
where the time goes in v2:
time: 203 us
  waiting for transfers between devices  108 us (53%)
  matrix products  37 us (18%)
  blocking collectives  15.6 us (8%)
  local copies, waits for them, and re-layouts  15.5 us (8%)
  between operations  13.3 us (7%)
  other arithmetic  7.66 us (4%)
  starting transfers between devices  4.99 us (2%)
    reduce_scatter x2, waiting for transfers between devices, on_device(): lax.psum_scatter(own, 'expert', scatter_dimension=0, tiled=True)  57.2 us
    all_gather x1, waiting for transfers between devices, on_device(): combined = lax.all_gather(combined, 'expert', axis=0, tiled=True)  37.9 us
    all_gather x1, blocking collectives, on_device(): routed = lax.all_gather(routed, 'expert', axis=0, tiled=True)  15.6 us
    dot_general x2, matrix products, on_device(): jnp.einsum('esf,edf->esd', gathered, weights, preferred_element_type=jnp....  15.1 us
    dot_general x2, matrix products, on_device(): own = jnp.dot(spread, partial_value, preferred_element_type=jnp.float32)  9.06 us
    dot_general x1, matrix products, on_device(): return jnp.dot(columns, combined, preferred_element_type=jnp.float32)  8.37 us
    unnamed x17, local copies, waits for them, and re-layouts  7.69 us
    all_to_all x1, waiting for transfers between devices, on_device(): lax.all_to_all(turned, 'expert', split_axis=0, concat_axis=0, tiled=True)  7.07 us
  transfers between devices with their start and end apart: 5, of which 5 were waited for; matrix products, arithmetic and copies ran while one was open for 25% of the time, Pallas kernels for 0%

profile of v2, /device:TPU:0, one launch (start us, length us, event | category | flops | bytes accessed | tf_op | source)
XLA Modules:
  0.0 202.6 jit_solution(4831141342094842734)
XLA Ops:
  6.5 0.7 all-gather.3.cloned.1.call-update
  7.3 3.9 %copy.19 = bf16[128,7168]{0,1:T(8,128)(2,1)} copy(bf16[128,7168]{1,0:T(8,128)(2,1)} %param.7) | data formatting | bytes 3670016 | tf_op args[0]
  11.2 15.6 %all_gather.10 = f32[1024,16]{0,1:T(8,128)S(1)} all-gather(f32[128,16]{0,1:T(8,128)S(1)} %pad_maximum_fusion), channel_id=1, replica_groups=mesh['dp'=4,'expert'=8] {'expert'}, dimensions={0}, use_global_device_ids=true | all-gather | bytes 73728 | tf_op jit(solution)/shard_map/all_gather | solution.py:38
  26.8 4.7 %all-to-all-start = ((bf16[8,896,128]{2,1,0:T(8,128)(2,1)}), bf16[8,896,128]{2,1,0:T(8,128)(2,1)}, u32[]{:S(2)}, u32[]{:S(2)}) async-start(bf16[8,896,128]{2,1,0:T(8,128)(2,1)} %bitcast.1), calls=%async_computation | async-start | bytes 3670016 | tf_op jit(solution)/shard_map/all_to_all | solution.py:41
  31.5 0.0 reduce-scatter.3.cloned.1.call-start
  31.5 0.1 compare_reduce_fusion
  31.7 0.1 fusion.10
  31.9 0.2 copy.20
  32.1 1.4 eq.36
  33.5 3.2 %copy.25 = s32[128,8,4,384]{3,1,2,0:T(8,128)} copy(s32[128,8,4,384]{3,2,1,0:T(4,128)S(1)} %bitcast.39) | data formatting | bytes 12582912
  36.7 0.1 fusion.11
  36.8 0.2 copy.21
  37.0 3.0 %broadcast_in_dim.42 = bf16[1024,4,384]{2,1,0:T(4,128)(2,1)S(1)} broadcast(bf16[1024,4]{1,0:T(8,128)(2,1)S(1)} %copy.21), dimensions={0,1} | broadcast | bytes 3153920 | tf_op jit(solution)/shard_map/jit(_where)/broadcast_in_dim | solution.py:22
  40.0 0.6 copy.26
  40.6 4.3 %fusion.21 = f32[128,1792]{1,0:T(8,128)} fusion(bf16[128,1024]{1,0:T(8,128)(2,1)S(1)} %copy-done, bf16[1792,1024]{1,0:T(8,128)(2,1)} %param.13), kind=kOutput, calls=%fused_computation.32 | convolution fusion | flops 469762048 | bytes 4849664 | tf_op jit(solution)/shard_map/tf,df->td/dot_general | solution.py:47
  44.9 5.5 %select_convert_fusion = bf16[1024,1536]{1,0:T(8,128)(2,1)} fusion(bf16[1024,1536]{1,0:T(8,128)(2,1)S(1)} %bitcast.42, s32[1024,1536]{1,0:T(8,128)} %bitcast.40, s32[1536]{0:T(1024)S(1)} %eq.39), kind=kLoop, calls=%fused_computation.4 | loop fusion | flops 3145728 | bytes 12589056 | tf_op jit(solution)/shard_map/convert_element_type | solution.py:23
  50.4 5.5 %all-gather.3.cloned.1.call-done = bf16[4,384,1024]{2,1,0:T(8,128)(2,1)} async-done(((bf16[4,96,1024]{2,1,0:T(8,128)(2,1)}), bf16[4,384,1024]{2,1,0:T(8,128)(2,1)}) %all-gather.3.cloned.1.call-update) | async-done | bytes 3145744 | tf_op jit(solution)/shard_map/all_gather | solution.py:36
  55.9 7.5 %fusion.4 = bf16[4,384,896]{2,1,0:T(8,128)(2,1)S(1)} fusion(bf16[4,384,1024]{2,1,0:T(8,128)(2,1)} %all-gather.3.cloned.1.call-done, bf16[4,1792,1024]{2,1,0:T(8,128)(2,1)} %param.11), kind=kOutput, calls=%fused_computation.5 | convolution fusion | flops 2819948544 | bytes 13238272 | tf_op jit(solution)/shard_map/esf,edf->esd/dot_general | solution.py:57
  63.4 4.5 %convolution_convert_fusion.1 = bf16[1024,896]{1,0:T(8,128)(2,1)} fusion(bf16[1024,1536]{1,0:T(8,128)(2,1)S(1)} %copy-done.3, bf16[1536,896]{1,0:T(8,128)(2,1)S(1)} %bitcast.46), kind=kOutput, calls=%fused_computation.8 | convolution fusion | flops 2819489792 | bytes 7733248 | tf_op jit(solution)/shard_map/dot_general | solution.py:61
  68.0 7.1 %all-to-all-done = bf16[8,896,128]{2,1,0:T(8,128)(2,1)} async-done(((bf16[8,896,128]{2,1,0:T(8,128)(2,1)}), bf16[8,896,128]{2,1,0:T(8,128)(2,1)}, u32[]{:S(2)}, u32[]{:S(2)}) %all-to-all-start) | async-done | bytes 1835040 | tf_op jit(solution)/shard_map/all_to_all | solution.py:41
  75.0 0.0 reduce-scatter.3.cloned.1.call-update
  75.1 0.2 reduce-scatter.5.cloned.1.call-start
  75.3 7.6 %fusion.7 = bf16[4,384,896]{2,1,0:T(8,128)(2,1)S(1)} fusion(bf16[4,384,1024]{2,1,0:T(8,128)(2,1)} %all-gather.3.cloned.1.call-done, bf16[4,1792,1024]{2,1,0:T(8,128)(2,1)} %param.11), kind=kOutput, calls=%fused_computation.6 | convolution fusion | flops 2819948544 | bytes 13238272 | tf_op jit(solution)/shard_map/esf,edf->esd/dot_general | solution.py:57
  82.9 4.5 %convolution_convert_fusion = bf16[1024,896]{1,0:T(8,128)(2,1)} fusion(bf16[1024,1536]{1,0:T(8,128)(2,1)S(1)} %copy-done.4, bf16[1536,896]{1,0:T(8,128)(2,1)S(1)} %bitcast.45), kind=kOutput, calls=%fused_computation.7 | convolution fusion | flops 2819489792 | bytes 7733248 | tf_op jit(solution)/shard_map/dot_general | solution.py:61
  87.5 0.0 reduce-scatter.5.cloned.1.call-update
  87.5 0.0 all-gather.5.cloned.1.call-start
  87.5 21.7 %reduce-scatter.3.cloned.1.call-done = bf16[128,896]{1,0:T(8,128)(2,1)} async-done(((bf16[1024,896]{1,0:T(8,128)(2,1)}), bf16[128,896]{1,0:T(8,128)(2,1)}) %reduce-scatter.3.cloned.1.call-update) | async-done | bytes 229392 | tf_op jit(solution)/shard_map/reduce_scatter | solution.py:65
  109.2 35.5 %reduce-scatter.5.cloned.1.call-done = bf16[128,896]{1,0:T(8,128)(2,1)} async-done(((bf16[1024,896]{1,0:T(8,128)(2,1)}), bf16[128,896]{1,0:T(8,128)(2,1)}) %reduce-scatter.5.cloned.1.call-update) | async-done | bytes 229392 | tf_op jit(solution)/shard_map/reduce_scatter | solution.py:65
  144.7 1.9 add_convert_fusion
  146.7 3.1 %copy.22 = bf16[896,8,128]{0,2,1:T(8,128)(2,1)S(1)} copy(bf16[896,8,128]{2,0,1:T(8,128)(2,1)} %bitcast.5) | data formatting | bytes 3670016 | tf_op jit(solution)/shard_map/transpose | solution.py:66
  149.7 37.9 %all-gather.5.cloned.1.call-done = bf16[1024,1792]{1,0:T(8,128)(2,1)} async-done(((bf16[128,1792]{1,0:T(8,128)(2,1)}), bf16[1024,1792]{1,0:T(8,128)(2,1)}) %all-gather.5.cloned.1.call-update) | async-done | bytes 3670032 | tf_op jit(solution)/shard_map/all_gather | solution.py:69
  187.6 8.4 %fusion.22 = f32[896,1792]{1,0:T(8,128)} fusion(bf16[896,1024]{0,1:T(8,128)(2,1)S(1)} %bitcast.43, bf16[1024,1792]{1,0:T(8,128)(2,1)} %all-gather.5.cloned.1.call-done), kind=kOutput, calls=%fused_computation.33 | convolution fusion | flops 3288334336 | bytes 11927552 | tf_op jit(solution)/shard_map/dot_general | solution.py:71
  (24 shorter events, 0.1 us)
Async XLA Ops:
  6.5 34.1 %copy-start = (bf16[128,1024]{1,0:T(8,128)(2,1)S(1)}, bf16[128,1024]{1,0:T(8,128)(2,1)}, u32[]{:S(2)}) copy-start(bf16[128,1024]{1,0:T(8,128)(2,1)} %param.12) | copy-start | bytes 786436
  6.5 4.6 %copy-start.5 = (s32[128,8]{0,1:T(8,128)S(1)}, s32[128,8]{0,1:T(8,128)}, u32[]{:S(2)}) copy-start(s32[128,8]{0,1:T(8,128)} %param.8) | copy-start | bytes 12292
  6.5 4.6 %copy-start.6 = (f32[128,8]{0,1:T(8,128)S(1)}, f32[128,8]{0,1:T(8,128)}, u32[]{:S(2)}) copy-start(f32[128,8]{0,1:T(8,128)} %param.9) | copy-start | bytes 12292
  6.5 49.4 %all-gather.3.cloned.1.call-start = ((), (), s32[]{:S(2)}) async-start(), calls=%async_computation.3 | async-start | bytes 3932160 | tf_op jit(solution)/shard_map/all_gather | solution.py:36
  26.8 48.2 %all-to-all-start = ((bf16[8,896,128]{2,1,0:T(8,128)(2,1)}), bf16[8,896,128]{2,1,0:T(8,128)(2,1)}, u32[]{:S(2)}, u32[]{:S(2)}) async-start(bf16[8,896,128]{2,1,0:T(8,128)(2,1)} %bitcast.1), calls=%async_computation | async-start | bytes 3670016 | tf_op jit(solution)/shard_map/all_to_all | solution.py:41
  31.5 77.8 %reduce-scatter.3.cloned.1.call-start = ((), (), s32[]{:S(2)}) async-start(), calls=%async_computation.4 | async-start | bytes 2064384 | tf_op jit(solution)/shard_map/reduce_scatter | solution.py:65
  50.4 13.0 %copy-start.3 = (bf16[1024,1536]{1,0:T(8,128)(2,1)S(1)}, bf16[1024,1536]{1,0:T(8,128)(2,1)}, u32[]{:S(2)}) copy-start(bf16[1024,1536]{1,0:T(8,128)(2,1)} %select_convert_fusion) | copy-start | bytes 9437188
  75.1 69.7 %reduce-scatter.5.cloned.1.call-start = ((), (), s32[]{:S(2)}) async-start(), calls=%async_computation.5 | async-start | bytes 2064384 | tf_op jit(solution)/shard_map/reduce_scatter | solution.py:65
  75.3 7.6 %copy-start.4 = (bf16[1024,1536]{1,0:T(8,128)(2,1)S(1)}, bf16[1024,1536]{1,0:T(8,128)(2,1)}, u32[]{:S(2)}) copy-start(bf16[1024,1536]{1,0:T(8,128)(2,1)} %select_convert_fusion) | copy-start | bytes 9437188
  82.9 61.8 %copy-start.2 = (f32[128,1792]{1,0:T(8,128)S(1)}, f32[128,1792]{1,0:T(8,128)}, u32[]{:S(2)}) copy-start(f32[128,1792]{1,0:T(8,128)} %fusion.21) | copy-start | bytes 2752516
  87.5 100.2 %all-gather.5.cloned.1.call-start = ((), (), s32[]{:S(2)}) async-start(), calls=%async_computation.6 | async-start | bytes 4128768 | tf_op jit(solution)/shard_map/all_gather | solution.py:69
  187.6 8.4 %copy-start.1 = (bf16[128,1024]{1,0:T(8,128)(2,1)S(1)}, bf16[128,1024]{1,0:T(8,128)(2,1)}, u32[]{:S(2)}) copy-start(bf16[128,1024]{1,0:T(8,128)(2,1)} %param.12) | copy-start | bytes 786436
Sparse Core Ops, SparseCore 0:
  9.2 46.6 all-gather.2
  75.2 34.0 reduce-scatter.2
  111.6 33.1 reduce-scatter.4
  146.8 40.8 all-gather.4

commit v3 on v2

--- a/solution.py
+++ b/solution.py
@@ -49,22 +49,14 @@
     )
     gathered, spread, shared_term = lax.optimization_barrier((gathered, spread, shared_term))
 
-    parts = 2 if feature_block % 256 == 0 else 1
-    step = feature_block // parts
-    sums = []
-    for part in range(parts):
-        weights = expert_weights[:, part * step : (part + 1) * step]
-        partial_value = jnp.einsum(
-            "esf,edf->esd", gathered, weights, preferred_element_type=jnp.float32
-        ).astype(jnp.bfloat16)
-        partial_value = partial_value.reshape(local_experts * slot_total, step)
-        own = jnp.dot(spread, partial_value, preferred_element_type=jnp.float32)
-        own = own.astype(jnp.bfloat16)
-        if part == 0:
-            own, columns = lax.optimization_barrier((own, columns))
-        sums.append(lax.psum_scatter(own, "expert", scatter_dimension=0, tiled=True))
+    partial_value = jnp.einsum(
+        "esf,edf->esd", gathered, expert_weights, preferred_element_type=jnp.float32
+    ).astype(jnp.bfloat16)
+    partial_value = partial_value.reshape(local_experts * slot_total, feature_block)
+    own = jnp.dot(spread, partial_value, preferred_element_type=jnp.float32)
+    own, columns = lax.optimization_barrier((own.astype(jnp.bfloat16), columns))
+    summed = lax.psum_scatter(own, "expert", scatter_dimension=0, tiled=True)
     columns = columns.transpose(1, 0, 2).reshape(rows, groups * block)
-    summed = jnp.concatenate(sums, axis=1)
     combined = (summed.astype(jnp.float32) + shared_term).astype(jnp.bfloat16)
     combined = lax.all_gather(combined, "expert", axis=0, tiled=True)
     columns, combined = lax.optimization_barrier((columns, combined))

time: 203 us -> 187 us (0.921)
  waiting for transfers between devices: 108 us -> 92.1 us
    reduce_scatter x2 -> x1, waiting for transfers between devices: 57.2 us -> 45 us  [on_device(): summed = lax.psum_scatter(own, 'expert', scatter_dimension=0, tiled=True)]
    all_to_all x1, waiting for transfers between devices: 7.07 us -> 0.01 us  [on_device(): lax.all_to_all(turned, 'expert', split_axis=0, concat_axis=0, tiled=True)]
    dot_general x1, matrix products: 4.31 us -> 1.33 us  [on_device(): jnp.einsum('tf,df->td', shared_grads, shared_weight, preferred_element_ty...]
    all_gather x1, waiting for transfers between devices: 5.52 us -> 8.32 us  [on_device(): gathered = lax.all_gather(slot_grads, 'dp', axis=1, tiled=True)]
    dot_general x2 -> x1, matrix products: 15.1 us -> 17.1 us  [on_device(): jnp.einsum('esf,edf->esd', gathered, expert_weights, preferred_element_ty...]
    dot_general x2 -> x1, matrix products: 9.06 us -> 10.3 us  [on_device(): own = jnp.dot(spread, partial_value, preferred_element_type=jnp.float32)]
    unnamed x17 -> x13, local copies, waits for them, and re-layouts: 7.69 us -> 7.67 us
  transfers between devices with their start and end apart: 5 -> 4, of which waited for: 5 -> 3; matrix products, arithmetic and copies ran while one was open for 25% -> 27% of each run, Pallas kernels for 0% -> 0%
where the time goes in v3:
time: 187 us; the launch traced here: 186 us
  waiting for transfers between devices  92.1 us (49%)
  matrix products  37.2 us (20%)
  blocking collectives  15.6 us (8%)
  local copies, waits for them, and re-layouts  15.5 us (8%)
  between operations  13.2 us (7%)
  other arithmetic  7.81 us (4%)
  starting transfers between devices  4.94 us (3%)
    reduce_scatter x1, waiting for transfers between devices, on_device(): summed = lax.psum_scatter(own, 'expert', scatter_dimension=0, tiled=True)  45 us
    all_gather x1, waiting for transfers between devices, on_device(): combined = lax.all_gather(combined, 'expert', axis=0, tiled=True)  38 us
    dot_general x1, matrix products, on_device(): jnp.einsum('esf,edf->esd', gathered, expert_weights, preferred_element_ty...  17.1 us
    all_gather x1, blocking collectives, on_device(): routed = lax.all_gather(routed, 'expert', axis=0, tiled=True)  15.6 us
    dot_general x1, matrix products, on_device(): own = jnp.dot(spread, partial_value, preferred_element_type=jnp.float32)  10.3 us
    dot_general x1, matrix products, on_device(): return jnp.dot(columns, combined, preferred_element_type=jnp.float32)  8.37 us
    all_gather x1, waiting for transfers between devices, on_device(): gathered = lax.all_gather(slot_grads, 'dp', axis=1, tiled=True)  8.32 us
    unnamed x13, local copies, waits for them, and re-layouts  7.67 us
  transfers between devices with their start and end apart: 4, of which 3 were waited for; matrix products, arithmetic and copies ran while one was open for 27% of the time, Pallas kernels for 0%

profile of v3, /device:TPU:0, one launch (start us, length us, event | category | flops | bytes accessed | tf_op | source)
XLA Modules:
  0.0 186.5 jit_solution(11790562630573423977)
XLA Ops:
  6.5 0.0 copy-start
  6.5 0.0 all-gather.3.cloned.1.call-start
  6.5 0.7 all-gather.3.cloned.1.call-update
  7.3 3.9 %copy.19 = bf16[128,7168]{0,1:T(8,128)(2,1)} copy(bf16[128,7168]{1,0:T(8,128)(2,1)} %param.7) | data formatting | bytes 3670016 | tf_op args[0]
  11.2 15.6 %all_gather.10 = f32[1024,16]{0,1:T(8,128)S(1)} all-gather(f32[128,16]{0,1:T(8,128)S(1)} %pad_maximum_fusion), channel_id=1, replica_groups=mesh['dp'=4,'expert'=8] {'expert'}, dimensions={0}, use_global_device_ids=true | all-gather | bytes 73728 | tf_op jit(solution)/shard_map/all_gather | solution.py:38
  26.8 4.7 %all-to-all-start = ((bf16[8,896,128]{2,1,0:T(8,128)(2,1)}), bf16[8,896,128]{2,1,0:T(8,128)(2,1)}, u32[]{:S(2)}, u32[]{:S(2)}) async-start(bf16[8,896,128]{2,1,0:T(8,128)(2,1)} %bitcast.1), calls=%async_computation | async-start | bytes 3670016 | tf_op jit(solution)/shard_map/all_to_all | solution.py:41
  31.5 0.0 reduce-scatter.2.cloned.1.call-start
  31.5 0.1 compare_reduce_fusion
  31.7 0.1 fusion
  31.8 0.2 copy.20
  32.1 1.4 eq.36
  33.5 3.2 %copy.25 = s32[128,8,4,384]{3,1,2,0:T(8,128)} copy(s32[128,8,4,384]{3,2,1,0:T(4,128)S(1)} %bitcast.36) | data formatting | bytes 12582912
  36.7 0.1 fusion.1
  36.8 0.2 copy.21
  37.0 3.0 %broadcast_in_dim.42 = bf16[1024,4,384]{2,1,0:T(4,128)(2,1)S(1)} broadcast(bf16[1024,4]{1,0:T(8,128)(2,1)S(1)} %copy.21), dimensions={0,1} | broadcast | bytes 3153920 | tf_op jit(solution)/shard_map/jit(_where)/broadcast_in_dim | solution.py:22
  40.0 0.6 copy.26
  40.6 0.0 copy-start.2
  40.6 5.7 %select_convert_fusion = bf16[1024,1536]{1,0:T(8,128)(2,1)} fusion(bf16[1024,1536]{1,0:T(8,128)(2,1)S(1)} %bitcast.39, s32[1024,1536]{1,0:T(8,128)} %bitcast.37, s32[1536]{0:T(1024)S(1)} %eq.39), kind=kLoop, calls=%fused_computation | loop fusion | flops 3145728 | bytes 12589056 | tf_op jit(solution)/shard_map/convert_element_type | solution.py:23
  46.3 0.0 copy-done
  46.3 1.3 fusion.11
  47.6 8.3 %all-gather.3.cloned.1.call-done = bf16[4,384,1024]{2,1,0:T(8,128)(2,1)} async-done(((bf16[4,96,1024]{2,1,0:T(8,128)(2,1)}), bf16[4,384,1024]{2,1,0:T(8,128)(2,1)}) %all-gather.3.cloned.1.call-update) | async-done | bytes 3145744 | tf_op jit(solution)/shard_map/all_gather | solution.py:36
  55.9 17.1 %convolution_convert_fusion = bf16[4,384,1792]{2,1,0:T(8,128)(2,1)} fusion(bf16[4,384,1024]{2,1,0:T(8,128)(2,1)} %all-gather.3.cloned.1.call-done, bf16[4,1792,1024]{2,1,0:T(8,128)(2,1)} %param.11), kind=kOutput, calls=%fused_computation.1 | convolution fusion | flops 5639897088 | bytes 23330816 | tf_op jit(solution)/shard_map/esf,edf->esd/dot_general | solution.py:52
  73.0 10.3 %convolution_convert_fusion.1 = bf16[1024,1792]{1,0:T(8,128)(2,1)} fusion(bf16[1024,1536]{1,0:T(8,128)(2,1)} %select_convert_fusion, bf16[1536,1792]{1,0:T(8,128)(2,1)} %bitcast.42), kind=kOutput, calls=%fused_computation.2 | convolution fusion | flops 5638979584 | bytes 12320768 | tf_op jit(solution)/shard_map/dot_general | solution.py:56
  83.3 0.0 all-to-all-done
  83.3 0.0 reduce-scatter.2.cloned.1.call-update
  83.3 0.2 all-gather.5.cloned.1.call-start
  83.6 45.0 %reduce-scatter.2.cloned.1.call-done = bf16[128,1792]{1,0:T(8,128)(2,1)} async-done(((bf16[1024,1792]{1,0:T(8,128)(2,1)}), bf16[128,1792]{1,0:T(8,128)(2,1)}) %reduce-scatter.2.cloned.1.call-update) | async-done | bytes 458768 | tf_op jit(solution)/shard_map/reduce_scatter | solution.py:58
  128.6 1.9 add_convert_fusion
  130.4 0.0 all-gather.5.cloned.1.call-update
  130.5 3.1 %copy.22 = bf16[896,8,128]{0,2,1:T(8,128)(2,1)S(1)} copy(bf16[896,8,128]{2,0,1:T(8,128)(2,1)} %bitcast.5) | data formatting | bytes 3670016 | tf_op jit(solution)/shard_map/transpose | solution.py:59
  133.5 38.0 %all-gather.5.cloned.1.call-done = bf16[1024,1792]{1,0:T(8,128)(2,1)} async-done(((bf16[128,1792]{1,0:T(8,128)(2,1)}), bf16[1024,1792]{1,0:T(8,128)(2,1)}) %all-gather.5.cloned.1.call-update) | async-done | bytes 3670032 | tf_op jit(solution)/shard_map/all_gather | solution.py:61
  171.6 8.4 %fusion.12 = f32[896,1792]{1,0:T(8,128)} fusion(bf16[896,1024]{0,1:T(8,128)(2,1)S(1)} %bitcast.40, bf16[1024,1792]{1,0:T(8,128)(2,1)} %all-gather.5.cloned.1.call-done), kind=kOutput, calls=%fused_computation.27 | convolution fusion | flops 3288334336 | bytes 11927552 | tf_op jit(solution)/shard_map/dot_general | solution.py:63
  (15 shorter events, 0.1 us)
Async XLA Ops:
  6.5 39.7 %copy-start = (bf16[128,1024]{1,0:T(8,128)(2,1)S(1)}, bf16[128,1024]{1,0:T(8,128)(2,1)}, u32[]{:S(2)}) copy-start(bf16[128,1024]{1,0:T(8,128)(2,1)} %param.12) | copy-start | bytes 786436
  6.5 4.6 %copy-start.3 = (s32[128,8]{0,1:T(8,128)S(1)}, s32[128,8]{0,1:T(8,128)}, u32[]{:S(2)}) copy-start(s32[128,8]{0,1:T(8,128)} %param.8) | copy-start | bytes 12292
  6.5 4.6 %copy-start.4 = (f32[128,8]{0,1:T(8,128)S(1)}, f32[128,8]{0,1:T(8,128)}, u32[]{:S(2)}) copy-start(f32[128,8]{0,1:T(8,128)} %param.9) | copy-start | bytes 12292
  6.5 49.4 %all-gather.3.cloned.1.call-start = ((), (), s32[]{:S(2)}) async-start(), calls=%async_computation.2 | async-start | bytes 3932160 | tf_op jit(solution)/shard_map/all_gather | solution.py:36
  26.8 56.5 %all-to-all-start = ((bf16[8,896,128]{2,1,0:T(8,128)(2,1)}), bf16[8,896,128]{2,1,0:T(8,128)(2,1)}, u32[]{:S(2)}, u32[]{:S(2)}) async-start(bf16[8,896,128]{2,1,0:T(8,128)(2,1)} %bitcast.1), calls=%async_computation | async-start | bytes 3670016 | tf_op jit(solution)/shard_map/all_to_all | solution.py:41
  31.5 97.1 %reduce-scatter.2.cloned.1.call-start = ((), (), s32[]{:S(2)}) async-start(), calls=%async_computation.3 | async-start | bytes 4128768 | tf_op jit(solution)/shard_map/reduce_scatter | solution.py:58
  40.6 5.7 %copy-start.2 = (bf16[1792,1024]{1,0:T(8,128)(2,1)S(1)}, bf16[1792,1024]{1,0:T(8,128)(2,1)}, u32[]{:S(2)}) copy-start(bf16[1792,1024]{1,0:T(8,128)(2,1)} %param.13) | copy-start | bytes 11010052
  83.3 88.2 %all-gather.5.cloned.1.call-start = ((), (), s32[]{:S(2)}) async-start(), calls=%async_computation.4 | async-start | bytes 4128768 | tf_op jit(solution)/shard_map/all_gather | solution.py:61
  171.6 8.4 %copy-start.1 = (bf16[128,1024]{1,0:T(8,128)(2,1)S(1)}, bf16[128,1024]{1,0:T(8,128)(2,1)}, u32[]{:S(2)}) copy-start(bf16[128,1024]{1,0:T(8,128)(2,1)} %param.12) | copy-start | bytes 786436
Sparse Core Ops, SparseCore 0:
  9.2 46.6 all-gather.2
  83.5 45.0 reduce-scatter.1
  130.6 40.9 all-gather.4

commit v4 on v3

--- a/solution.py
+++ b/solution.py
@@ -4,7 +4,7 @@
 from jax.sharding import PartitionSpec as P
 
 
-def source_matrix(ids, gates, first, local_experts, groups, capacity):
+def source_matrix(ids, gates, first, local_experts, groups, capacity, slots):
     tokens = ids.shape[0]
     block = tokens // groups
     experts = first + jnp.arange(local_experts, dtype=jnp.int32)
@@ -18,7 +18,6 @@
     place = place.astype(jnp.int32).reshape(tokens, local_experts)
     source = (jnp.arange(tokens, dtype=jnp.int32) // block)[:, None]
     slot = jnp.where(named, source * capacity + place, -1)
-    slots = jnp.arange(groups * capacity, dtype=jnp.int32)
     spread = jnp.where(slot[:, :, None] == slots[None, None, :], gate[:, :, None], 0.0)
     return spread.astype(jnp.bfloat16).reshape(tokens, local_experts * groups * capacity)
 
@@ -33,7 +32,14 @@
     block, width = activations.shape
     rows = width // groups
 
-    gathered = lax.all_gather(slot_grads, "dp", axis=1, tiled=True)
+    shard, peers = slot_grads.shape[1], lax.axis_size("dp")
+    pieces = [slot_grads]
+    for turn in range(1, peers):
+        pairs = [(peer, peer ^ turn) for peer in range(peers)]
+        pieces.append(lax.ppermute(slot_grads, "dp", pairs))
+    owners = lax.axis_index("dp") ^ jnp.arange(peers, dtype=jnp.int32)
+    slots = owners[:, None] * shard + jnp.arange(shard, dtype=jnp.int32)[None, :]
+    slots = slots.reshape(-1)
     routed = jnp.concatenate([expert_ids.astype(jnp.float32), gate_weights], axis=1)
     routed = lax.all_gather(routed, "expert", axis=0, tiled=True)
     turned = activations.T.reshape(groups, rows, block)
@@ -43,10 +49,11 @@
     top = expert_ids.shape[1]
     ids, gates = routed[:, :top].astype(jnp.int32), routed[:, top:]
     first = lax.axis_index("expert") * local_experts
-    spread = source_matrix(ids, gates, first, local_experts, groups, capacity)
+    spread = source_matrix(ids, gates, first, local_experts, groups, capacity, slots)
     shared_term = jnp.einsum(
         "tf,df->td", shared_grads, shared_weight, preferred_element_type=jnp.float32
     )
+    gathered = jnp.concatenate(pieces, axis=1)
     gathered, spread, shared_term = lax.optimization_barrier((gathered, spread, shared_term))
 
     partial_value = jnp.einsum(

time: 187 us -> 186 us (level)
  waiting for transfers between devices: 92.1 us -> 84.5 us
  starting transfers between devices: 4.94 us -> 9.41 us
  other arithmetic: 7.81 us -> 10.9 us
    all_gather x1 -> x0, waiting for transfers between devices: 8.32 us -> none  [on_device(): gathered = lax.all_gather(slot_grads, 'dp', axis=1, tiled=True)]
    ppermute x0 -> x3, starting transfers between devices: none -> 4.47 us  [on_device(): pieces.append(lax.ppermute(slot_grads, 'dp', pairs))]
    concatenate x0 -> x1, other arithmetic: none -> 2.99 us  [on_device(): gathered = jnp.concatenate(pieces, axis=1)]
    unnamed x13 -> x15, local copies, waits for them, and re-layouts: 7.67 us -> 7.67 us
  transfers between devices with their start and end apart: 4 -> 6, of which waited for: 3 -> 2; matrix products, arithmetic and copies ran while one was open for 27% -> 29% of each run, Pallas kernels for 0% -> 0%
where the time goes in v4:
time: 186 us
  waiting for transfers between devices  84.5 us (45%)
  matrix products  37.3 us (20%)
  local copies, waits for them, and re-layouts  15.6 us (8%)
  blocking collectives  14.6 us (8%)
  between operations  13.6 us (7%)
  other arithmetic  10.9 us (6%)
  starting transfers between devices  9.41 us (5%)
    reduce_scatter x1, waiting for transfers between devices, on_device(): summed = lax.psum_scatter(own, 'expert', scatter_dimension=0, tiled=True)  46.4 us
    all_gather x1, waiting for transfers between devices, on_device(): combined = lax.all_gather(combined, 'expert', axis=0, tiled=True)  38 us
    dot_general x1, matrix products, on_device(): jnp.einsum('esf,edf->esd', gathered, expert_weights, preferred_element_ty...  17.1 us
    all_gather x1, blocking collectives, on_device(): routed = lax.all_gather(routed, 'expert', axis=0, tiled=True)  14.6 us
    dot_general x1, matrix products, on_device(): own = jnp.dot(spread, partial_value, preferred_element_type=jnp.float32)  10.4 us
    dot_general x1, matrix products, on_device(): return jnp.dot(columns, combined, preferred_element_type=jnp.float32)  8.37 us
    unnamed x15, local copies, waits for them, and re-layouts  7.67 us
    convert_element_type x1, other arithmetic, source_matrix(): spread.astype(jnp.bfloat16)  5.66 us
  transfers between devices with their start and end apart: 6, of which 2 were waited for; matrix products, arithmetic and copies ran while one was open for 29% of the time, Pallas kernels for 0%

profile of v4, /device:TPU:0, one launch (start us, length us, event | category | flops | bytes accessed | tf_op | source)
XLA Modules:
  0.0 185.9 jit_solution(16765304774011780024)
XLA Ops:
  6.5 2.9 %collective-permute-start = (bf16[4,96,1024]{2,1,0:T(8,128)(2,1)}, bf16[4,96,1024]{2,1,0:T(8,128)(2,1)}, u32[]{:S(2)}, u32[]{:S(2)}) collective-permute-start(bf16[4,96,1024]{2,1,0:T(8,128)(2,1)} %param.10), channel_id=1, source_target_pairs={{0,8},{8,0},{16,24},{24,16},{1,9},{9,1},{17,25},{25,17},{2,10},{10... | collective-permute-start | bytes 2359304 | tf_op jit(solution)/shard_map/ppermute | solution.py:39
  9.5 1.5 collective-permute-start.1
  11.0 0.0 collective-permute-start.2
  11.0 3.9 %copy.19 = bf16[128,7168]{0,1:T(8,128)(2,1)} copy(bf16[128,7168]{1,0:T(8,128)(2,1)} %param.7) | data formatting | bytes 3670016 | tf_op args[0]
  14.9 14.6 %all_gather.6 = f32[1024,16]{0,1:T(8,128)S(1)} all-gather(f32[128,16]{0,1:T(8,128)S(1)} %pad_maximum_fusion.1), channel_id=1, replica_groups=mesh['dp'=4,'expert'=8] {'expert'}, dimensions={0}, use_global_device_ids=true | all-gather | bytes 73728 | tf_op jit(solution)/shard_map/all_gather | solution.py:44
  29.5 4.7 %all-to-all-start = ((bf16[8,896,128]{2,1,0:T(8,128)(2,1)}), bf16[8,896,128]{2,1,0:T(8,128)(2,1)}, u32[]{:S(2)}, u32[]{:S(2)}) async-start(bf16[8,896,128]{2,1,0:T(8,128)(2,1)} %bitcast.1), calls=%async_computation | async-start | bytes 3670016 | tf_op jit(solution)/shard_map/all_to_all | solution.py:47
  34.2 0.0 reduce-scatter.2.cloned.1.call-start
  34.3 0.1 compare_reduce_fusion
  34.4 0.1 fusion
  34.6 0.2 copy.20
  34.8 1.4 eq.36
  36.2 3.2 %copy.25 = s32[128,8,4,384]{3,1,2,0:T(8,128)} copy(s32[128,8,4,384]{3,2,1,0:T(4,128)S(1)} %bitcast.36) | data formatting | bytes 12582912
  39.5 0.1 fusion.1
  39.6 0.2 copy.21
  39.8 3.0 %broadcast_in_dim.43 = bf16[1024,4,384]{2,1,0:T(4,128)(2,1)S(1)} broadcast(bf16[1024,4]{1,0:T(8,128)(2,1)S(1)} %copy.21), dimensions={0,1} | broadcast | bytes 3153920 | tf_op jit(solution)/shard_map/jit(_where)/broadcast_in_dim | solution.py:21
  42.8 0.6 copy.26
  43.3 0.1 iota_add_fusion
  43.4 0.1 add.59
  43.5 5.7 %select_convert_fusion = bf16[1024,1536]{1,0:T(8,128)(2,1)} fusion(bf16[1024,1536]{1,0:T(8,128)(2,1)S(1)} %bitcast.39, s32[1024,1536]{1,0:T(8,128)} %bitcast.37, s32[1536]{0:T(1024)S(1)} %eq.39), kind=kLoop, calls=%fused_computation | loop fusion | flops 3145728 | bytes 12589056 | tf_op jit(solution)/shard_map/convert_element_type | solution.py:22
  49.2 1.3 fusion.11
  50.5 0.0 collective-permute-done
  50.6 3.0 %pad_maximum_fusion = bf16[4,384,1024]{2,1,0:T(8,128)(2,1)} fusion(bf16[4,96,1024]{2,1,0:T(8,128)(2,1)} %collective-permute-done.2, bf16[4,96,1024]{2,1,0:T(8,128)(2,1)} %collective-permute-done.1, bf16[4,96,1024]{2,1,0:T(8,128)(2,1)} %collective-permute-done, bf16[4,96,1024]{2,1,0:T(8,128)(2,1)S(1)} %copy-done.3), kind=kLoop, calls=%fused_computation.3 | loop fusion | flops 12582912 | bytes 6291456 | tf_op jit(solution)/shard_map/concatenate | solution.py:56
  53.6 17.1 %convolution_convert_fusion = bf16[4,384,1792]{2,1,0:T(8,128)(2,1)} fusion(bf16[4,384,1024]{2,1,0:T(8,128)(2,1)} %pad_maximum_fusion, bf16[4,1792,1024]{2,1,0:T(8,128)(2,1)} %param.11), kind=kOutput, calls=%fused_computation.1 | convolution fusion | flops 5639897088 | bytes 23330816 | tf_op jit(solution)/shard_map/esf,edf->esd/dot_general | solution.py:59
  70.7 10.4 %convolution_convert_fusion.1 = bf16[1024,1792]{1,0:T(8,128)(2,1)} fusion(bf16[1024,1536]{1,0:T(8,128)(2,1)} %select_convert_fusion, bf16[1536,1792]{1,0:T(8,128)(2,1)} %bitcast.42), kind=kOutput, calls=%fused_computation.2 | convolution fusion | flops 5638979584 | bytes 12320768 | tf_op jit(solution)/shard_map/dot_general | solution.py:63
  81.0 0.0 reduce-scatter.2.cloned.1.call-update
  81.0 0.2 all-gather.2.cloned.1.call-start
  81.3 46.4 %reduce-scatter.2.cloned.1.call-done = bf16[128,1792]{1,0:T(8,128)(2,1)} async-done(((bf16[1024,1792]{1,0:T(8,128)(2,1)}), bf16[128,1792]{1,0:T(8,128)(2,1)}) %reduce-scatter.2.cloned.1.call-update) | async-done | bytes 458768 | tf_op jit(solution)/shard_map/reduce_scatter | solution.py:65
  127.7 1.9 %add_convert_fusion = bf16[128,1792]{1,0:T(8,128)(2,1)} fusion(f32[128,1792]{1,0:T(8,128)S(1)} %fusion.11, bf16[128,1792]{1,0:T(8,128)(2,1)} %reduce-scatter.2.cloned.1.call-done), kind=kLoop, calls=%fused_computation.6 | loop fusion | flops 688128 | bytes 1835008 | tf_op jit(solution)/shard_map/convert_element_type | solution.py:67
  129.5 0.0 all-gather.2.cloned.1.call-update
  129.6 3.1 %copy.22 = bf16[896,8,128]{0,2,1:T(8,128)(2,1)S(1)} copy(bf16[896,8,128]{2,0,1:T(8,128)(2,1)} %bitcast.5) | data formatting | bytes 3670016 | tf_op jit(solution)/shard_map/transpose | solution.py:66
  132.6 38.0 %all-gather.2.cloned.1.call-done = bf16[1024,1792]{1,0:T(8,128)(2,1)} async-done(((bf16[128,1792]{1,0:T(8,128)(2,1)}), bf16[1024,1792]{1,0:T(8,128)(2,1)}) %all-gather.2.cloned.1.call-update) | async-done | bytes 3670032 | tf_op jit(solution)/shard_map/all_gather | solution.py:68
  170.7 8.4 %fusion.12 = f32[896,1792]{1,0:T(8,128)} fusion(bf16[896,1024]{0,1:T(8,128)(2,1)S(1)} %bitcast.40, bf16[1024,1792]{1,0:T(8,128)(2,1)} %all-gather.2.cloned.1.call-done), kind=kOutput, calls=%fused_computation.30 | convolution fusion | flops 3288334336 | bytes 11927552 | tf_op jit(solution)/shard_map/dot_general | solution.py:70
  (24 shorter events, 0.1 us)
Async XLA Ops:
  6.5 42.6 %copy-start = (bf16[128,1024]{1,0:T(8,128)(2,1)S(1)}, bf16[128,1024]{1,0:T(8,128)(2,1)}, u32[]{:S(2)}) copy-start(bf16[128,1024]{1,0:T(8,128)(2,1)} %param.12) | copy-start | bytes 786436
  6.5 8.3 %copy-start.4 = (s32[128,8]{0,1:T(8,128)S(1)}, s32[128,8]{0,1:T(8,128)}, u32[]{:S(2)}) copy-start(s32[128,8]{0,1:T(8,128)} %param.8) | copy-start | bytes 12292
  6.5 8.4 %copy-start.5 = (f32[128,8]{0,1:T(8,128)S(1)}, f32[128,8]{0,1:T(8,128)}, u32[]{:S(2)}) copy-start(f32[128,8]{0,1:T(8,128)} %param.9) | copy-start | bytes 12292
  6.5 44.0 %collective-permute-start = (bf16[4,96,1024]{2,1,0:T(8,128)(2,1)}, bf16[4,96,1024]{2,1,0:T(8,128)(2,1)}, u32[]{:S(2)}, u32[]{:S(2)}) collective-permute-start(bf16[4,96,1024]{2,1,0:T(8,128)(2,1)} %param.10), channel_id=1, source_target_pairs={{0,8},{8,0},{16,24},{24,16},{1,9},{9,1},{17,25},{25,17},{2,10},{10... | collective-permute-start | bytes 2359304 | tf_op jit(solution)/shard_map/ppermute | solution.py:39
  9.5 41.1 %collective-permute-start.1 = (bf16[4,96,1024]{2,1,0:T(8,128)(2,1)}, bf16[4,96,1024]{2,1,0:T(8,128)(2,1)}, u32[]{:S(2)}, u32[]{:S(2)}) collective-permute-start(bf16[4,96,1024]{2,1,0:T(8,128)(2,1)} %param.10), channel_id=1, source_target_pairs={{0,16},{8,24},{16,0},{24,8},{1,17},{9,25},{17,1},{25,9},{2,18},{10... | collective-permute-start | bytes 2359304 | tf_op jit(solution)/shard_map/ppermute | solution.py:39
  11.0 39.5 %collective-permute-start.2 = (bf16[4,96,1024]{2,1,0:T(8,128)(2,1)}, bf16[4,96,1024]{2,1,0:T(8,128)(2,1)}, u32[]{:S(2)}, u32[]{:S(2)}) collective-permute-start(bf16[4,96,1024]{2,1,0:T(8,128)(2,1)} %param.10), channel_id=1, source_target_pairs={{0,24},{8,16},{16,8},{24,0},{1,25},{9,17},{17,9},{25,1},{2,26},{10... | collective-permute-start | bytes 2359304 | tf_op jit(solution)/shard_map/ppermute | solution.py:39
  29.5 51.5 %all-to-all-start = ((bf16[8,896,128]{2,1,0:T(8,128)(2,1)}), bf16[8,896,128]{2,1,0:T(8,128)(2,1)}, u32[]{:S(2)}, u32[]{:S(2)}) async-start(bf16[8,896,128]{2,1,0:T(8,128)(2,1)} %bitcast.1), calls=%async_computation | async-start | bytes 3670016 | tf_op jit(solution)/shard_map/all_to_all | solution.py:47
  34.2 93.4 %reduce-scatter.2.cloned.1.call-start = ((), (), s32[]{:S(2)}) async-start(), calls=%async_computation.2 | async-start | bytes 4128768 | tf_op jit(solution)/shard_map/reduce_scatter | solution.py:65
  43.5 5.7 %copy-start.2 = (bf16[1792,1024]{1,0:T(8,128)(2,1)S(1)}, bf16[1792,1024]{1,0:T(8,128)(2,1)}, u32[]{:S(2)}) copy-start(bf16[1792,1024]{1,0:T(8,128)(2,1)} %param.13) | copy-start | bytes 11010052
  49.2 1.4 copy-start.3
  81.0 89.6 %all-gather.2.cloned.1.call-start = ((), (), s32[]{:S(2)}) async-start(), calls=%async_computation.3 | async-start | bytes 4128768 | tf_op jit(solution)/shard_map/all_gather | solution.py:68
  170.7 8.4 %copy-start.1 = (bf16[128,1024]{1,0:T(8,128)(2,1)S(1)}, bf16[128,1024]{1,0:T(8,128)(2,1)}, u32[]{:S(2)}) copy-start(bf16[128,1024]{1,0:T(8,128)(2,1)} %param.12) | copy-start | bytes 786436
Sparse Core Ops, SparseCore 0:
  81.2 46.4 reduce-scatter.1
  129.7 40.9 all-gather.1

commit v5 on v4

--- a/solution.py
+++ b/solution.py
@@ -54,7 +54,7 @@
         "tf,df->td", shared_grads, shared_weight, preferred_element_type=jnp.float32
     )
     gathered = jnp.concatenate(pieces, axis=1)
-    gathered, spread, shared_term = lax.optimization_barrier((gathered, spread, shared_term))
+    gathered, shared_term = lax.optimization_barrier((gathered, shared_term))
 
     partial_value = jnp.einsum(
         "esf,edf->esd", gathered, expert_weights, preferred_element_type=jnp.float32

time: 186 us -> 182 us (0.978)
  local copies, waits for them, and re-layouts: 15.6 us -> 6.63 us
  waiting for transfers between devices: 84.5 us -> 91.1 us
  other arithmetic: 10.9 us -> 6.76 us
  matrix products: 37.3 us -> 39.9 us
    ppermute x3, waiting for transfers between devices: 0.01 us -> 5.76 us  [on_device(): pieces.append(lax.ppermute(slot_grads, 'dp', pairs))]
    convert_element_type x1 -> x0, other arithmetic: 5.66 us -> none  [source_matrix(): spread.astype(jnp.bfloat16)]
    unnamed x15 -> x3, local copies, waits for them, and re-layouts: 7.67 us -> 3.9 us
    broadcast_in_dim x1 -> x0, local copies, waits for them, and re-layouts: 2.97 us -> none  [source_matrix(): jnp.where(slot[:, :, None] == slots[None, None, :], gate[:, :, None], 0.0)]
    all_to_all x1, waiting for transfers between devices: 0.01 us -> 2.95 us  [on_device(): lax.all_to_all(turned, 'expert', split_axis=0, concat_axis=0, tiled=True)]
    reduce_scatter x1, waiting for transfers between devices: 46.4 us -> 43.9 us  [on_device(): summed = lax.psum_scatter(own, 'expert', scatter_dimension=0, tiled=True)]
    dot_general x1, matrix products: 1.33 us -> 3.36 us  [on_device(): jnp.einsum('tf,df->td', shared_grads, shared_weight, preferred_element_ty...]
  transfers between devices with their start and end apart: 6 -> 6, of which waited for: 2 -> 4; matrix products, arithmetic and copies ran while one was open for 29% -> 23% of each run, Pallas kernels for 0% -> 0%
where the time goes in v5:
time: 182 us
  waiting for transfers between devices  91.1 us (50%)
  matrix products  39.9 us (22%)
  blocking collectives  14.6 us (8%)
  between operations  13.5 us (7%)
  starting transfers between devices  9.4 us (5%)
  other arithmetic  6.76 us (4%)
  local copies, waits for them, and re-layouts  6.63 us (4%)
    reduce_scatter x1, waiting for transfers between devices, on_device(): summed = lax.psum_scatter(own, 'expert', scatter_dimension=0, tiled=True)  43.9 us
    all_gather x1, waiting for transfers between devices, on_device(): combined = lax.all_gather(combined, 'expert', axis=0, tiled=True)  38.5 us
    dot_general x1, matrix products, on_device(): jnp.einsum('esf,edf->esd', gathered, expert_weights, preferred_element_ty...  17.1 us
    all_gather x1, blocking collectives, on_device(): routed = lax.all_gather(routed, 'expert', axis=0, tiled=True)  14.6 us
    dot_general x1, matrix products, on_device(): own = jnp.dot(spread, partial_value, preferred_element_type=jnp.float32)  10.4 us
    dot_general x1, matrix products, on_device(): return jnp.dot(columns, combined, preferred_element_type=jnp.float32)  8.88 us
    ppermute x3, waiting for transfers between devices, on_device(): pieces.append(lax.ppermute(slot_grads, 'dp', pairs))  5.76 us
    all_to_all x1, starting transfers between devices, on_device(): lax.all_to_all(turned, 'expert', split_axis=0, concat_axis=0, tiled=True)  4.68 us
  transfers between devices with their start and end apart: 6, of which 4 were waited for; matrix products, arithmetic and copies ran while one was open for 23% of the time, Pallas kernels for 0%

profile of v5, /device:TPU:0, one launch (start us, length us, event | category | flops | bytes accessed | tf_op | source)
XLA Modules:
  0.0 181.9 jit_solution(14919773191886492902)
XLA Ops:
  6.5 0.0 copy-start
  6.5 3.0 %collective-permute-start.1 = (bf16[4,96,1024]{2,1,0:T(8,128)(2,1)}, bf16[4,96,1024]{2,1,0:T(8,128)(2,1)}, u32[]{:S(2)}, u32[]{:S(2)}) collective-permute-start(bf16[4,96,1024]{2,1,0:T(8,128)(2,1)} %param.10), channel_id=1, source_target_pairs={{0,16},{8,24},{16,0},{24,8},{1,17},{9,25},{17,1},{25,9},{2,18},{10... | collective-permute-start | bytes 2359304 | tf_op jit(solution)/shard_map/ppermute | solution.py:39
  9.5 1.5 collective-permute-start
  11.0 0.0 collective-permute-start.2
  11.0 0.7 convert_element_type.29
  11.7 0.7 pad_maximum_fusion.1
  12.4 14.6 %all_gather.6 = f32[1024,16]{0,1:T(8,128)S(1)} all-gather(f32[128,16]{0,1:T(8,128)S(1)} %pad_maximum_fusion.1), channel_id=1, replica_groups=mesh['dp'=4,'expert'=8] {'expert'}, dimensions={0}, use_global_device_ids=true | all-gather | bytes 73728 | tf_op jit(solution)/shard_map/all_gather | solution.py:44
  27.0 3.9 %copy.16 = bf16[128,7168]{0,1:T(8,128)(2,1)} copy(bf16[128,7168]{1,0:T(8,128)(2,1)} %param.7) | data formatting | bytes 3670016 | tf_op args[0]
  30.9 4.7 %all-to-all-start = ((bf16[8,896,128]{2,1,0:T(8,128)(2,1)}), bf16[8,896,128]{2,1,0:T(8,128)(2,1)S(1)}, u32[]{:S(2)}, u32[]{:S(2)}) async-start(bf16[8,896,128]{2,1,0:T(8,128)(2,1)} %bitcast.43), calls=%async_computation | async-start | bytes 3670016 | tf_op jit(solution)/shard_map/all_to_all | solution.py:47
  35.6 0.0 reduce-scatter.2.cloned.1.call-start
  35.7 0.1 iota_add_fusion
  35.7 0.1 compare_reduce_fusion
  35.9 0.1 fusion.10
  36.0 0.1 fusion.11
  36.2 0.1 add.59
  36.2 0.0 copy-done
  36.2 3.4 %fusion.22 = f32[128,1792]{1,0:T(8,128)S(1)} fusion(bf16[128,1024]{1,0:T(8,128)(2,1)S(1)} %copy-done, bf16[1792,1024]{1,0:T(8,128)(2,1)} %param.13), kind=kOutput, calls=%fused_computation.36 | convolution fusion | flops 469762048 | bytes 4849664 | tf_op jit(solution)/shard_map/tf,df->td/dot_general | solution.py:53
  39.6 0.0 collective-permute-done.1
  39.6 0.0 collective-permute-done
  39.6 5.8 %collective-permute-done.2 = bf16[4,96,1024]{2,1,0:T(8,128)(2,1)} collective-permute-done((bf16[4,96,1024]{2,1,0:T(8,128)(2,1)}, bf16[4,96,1024]{2,1,0:T(8,128)(2,1)}, u32[]{:S(2)}, u32[]{:S(2)}) %collective-permute-start.2) | collective-permute-done | bytes 786464 | tf_op jit(solution)/shard_map/ppermute | solution.py:39
  45.4 3.2 %pad_maximum_fusion = bf16[4,384,1024]{2,1,0:T(8,128)(2,1)} fusion(bf16[4,96,1024]{2,1,0:T(8,128)(2,1)} %collective-permute-done.2, bf16[4,96,1024]{2,1,0:T(8,128)(2,1)} %collective-permute-done.1, bf16[4,96,1024]{2,1,0:T(8,128)(2,1)} %collective-permute-done, bf16[4,96,1024]{2,1,0:T(8,128)(2,1)} %param.10), kind=kLoop, calls=%fused_computation.5 | loop fusion | flops 12582912 | bytes 6291456 | tf_op jit(solution)/shard_map/concatenate | solution.py:56
  48.6 17.1 %fusion.41 = bf16[4,384,1792]{2,1,0:T(8,128)(2,1)} fusion(bf16[4,384,1024]{2,1,0:T(8,128)(2,1)} %pad_maximum_fusion, bf16[4,1792,1024]{2,1,0:T(8,128)(2,1)} %param.11), kind=kOutput, calls=%fused_computation.3.clone.clone.clone.2 | convolution fusion | flops 5639897088 | bytes 23330816 | tf_op jit(solution)/shard_map/esf,edf->esd/dot_general | solution.py:59
  65.7 10.4 %bitcast_convert_fusion = bf16[1024,1792]{1,0:T(8,128)(2,1)} fusion(bf16[1024,4]{0,1:T(4,128)(2,1)S(1)} %fusion.11, s32[384]{0:T(512)S(1)} %add.59, s32[1024,4]{0,1:T(4,128)S(1)} %fusion.14, bf16[4,384,1792]{2,1,0:T(8,128)(2,1)} %fusion.41), kind=kOutput, calls=%fused_computation | convolution fusion | flops 5642125312 | bytes 9201152 | tf_op jit(solution)/shard_map/dot_general | solution.py:63
  76.1 3.0 %all-to-all-done = bf16[8,896,128]{2,1,0:T(8,128)(2,1)S(1)} async-done(((bf16[8,896,128]{2,1,0:T(8,128)(2,1)}), bf16[8,896,128]{2,1,0:T(8,128)(2,1)S(1)}, u32[]{:S(2)}, u32[]{:S(2)}) %all-to-all-start) | async-done | bytes 1835040 | tf_op jit(solution)/shard_map/all_to_all | solution.py:47
  79.0 0.0 reduce-scatter.2.cloned.1.call-update
  79.1 0.2 all-gather.2.cloned.1.call-start
  79.3 43.9 %reduce-scatter.2.cloned.1.call-done = bf16[128,1792]{1,0:T(8,128)(2,1)} async-done(((bf16[1024,1792]{1,0:T(8,128)(2,1)}), bf16[128,1792]{1,0:T(8,128)(2,1)}) %reduce-scatter.2.cloned.1.call-update) | async-done | bytes 458768 | tf_op jit(solution)/shard_map/reduce_scatter | solution.py:65
  123.2 1.9 %add_convert_fusion = bf16[128,1792]{1,0:T(8,128)(2,1)} fusion(f32[128,1792]{1,0:T(8,128)S(1)} %fusion.22, bf16[128,1792]{1,0:T(8,128)(2,1)} %reduce-scatter.2.cloned.1.call-done), kind=kLoop, calls=%fused_computation.12 | loop fusion | flops 688128 | bytes 1835008 | tf_op jit(solution)/shard_map/convert_element_type | solution.py:67
  125.1 0.0 all-gather.2.cloned.1.call-update
  125.1 2.6 %copy.17 = bf16[896,8,128]{0,2,1:T(8,128)(2,1)} copy(bf16[896,8,128]{2,0,1:T(8,128)(2,1)S(1)} %bitcast.42) | data formatting | bytes 3670016 | tf_op jit(solution)/shard_map/transpose | solution.py:66
  127.7 38.5 %all-gather.2.cloned.1.call-done = bf16[1024,1792]{1,0:T(8,128)(2,1)} async-done(((bf16[128,1792]{1,0:T(8,128)(2,1)}), bf16[1024,1792]{1,0:T(8,128)(2,1)}) %all-gather.2.cloned.1.call-update) | async-done | bytes 3670032 | tf_op jit(solution)/shard_map/all_gather | solution.py:68
  166.2 8.9 %fusion.23 = f32[896,1792]{1,0:T(8,128)} fusion(bf16[896,1024]{0,1:T(8,128)(2,1)} %bitcast.44, bf16[1024,1792]{1,0:T(8,128)(2,1)} %all-gather.2.cloned.1.call-done), kind=kOutput, calls=%fused_computation.37 | convolution fusion | flops 3288334336 | bytes 11927552 | tf_op jit(solution)/shard_map/dot_general | solution.py:70
  (5 shorter events, 0.1 us)
Async XLA Ops:
  6.5 29.7 %copy-start = (bf16[128,1024]{1,0:T(8,128)(2,1)S(1)}, bf16[128,1024]{1,0:T(8,128)(2,1)}, u32[]{:S(2)}) copy-start(bf16[128,1024]{1,0:T(8,128)(2,1)} %param.12) | copy-start | bytes 786436
  6.5 33.1 %collective-permute-start.1 = (bf16[4,96,1024]{2,1,0:T(8,128)(2,1)}, bf16[4,96,1024]{2,1,0:T(8,128)(2,1)}, u32[]{:S(2)}, u32[]{:S(2)}) collective-permute-start(bf16[4,96,1024]{2,1,0:T(8,128)(2,1)} %param.10), channel_id=1, source_target_pairs={{0,16},{8,24},{16,0},{24,8},{1,17},{9,25},{17,1},{25,9},{2,18},{10... | collective-permute-start | bytes 2359304 | tf_op jit(solution)/shard_map/ppermute | solution.py:39
  9.5 30.1 %collective-permute-start = (bf16[4,96,1024]{2,1,0:T(8,128)(2,1)}, bf16[4,96,1024]{2,1,0:T(8,128)(2,1)}, u32[]{:S(2)}, u32[]{:S(2)}) collective-permute-start(bf16[4,96,1024]{2,1,0:T(8,128)(2,1)} %param.10), channel_id=1, source_target_pairs={{0,8},{8,0},{16,24},{24,16},{1,9},{9,1},{17,25},{25,17},{2,10},{10... | collective-permute-start | bytes 2359304 | tf_op jit(solution)/shard_map/ppermute | solution.py:39
  11.0 34.4 %collective-permute-start.2 = (bf16[4,96,1024]{2,1,0:T(8,128)(2,1)}, bf16[4,96,1024]{2,1,0:T(8,128)(2,1)}, u32[]{:S(2)}, u32[]{:S(2)}) collective-permute-start(bf16[4,96,1024]{2,1,0:T(8,128)(2,1)} %param.10), channel_id=1, source_target_pairs={{0,24},{8,16},{16,8},{24,0},{1,25},{9,17},{17,9},{25,1},{2,26},{10... | collective-permute-start | bytes 2359304 | tf_op jit(solution)/shard_map/ppermute | solution.py:39
  30.9 48.1 %all-to-all-start = ((bf16[8,896,128]{2,1,0:T(8,128)(2,1)}), bf16[8,896,128]{2,1,0:T(8,128)(2,1)S(1)}, u32[]{:S(2)}, u32[]{:S(2)}) async-start(bf16[8,896,128]{2,1,0:T(8,128)(2,1)} %bitcast.43), calls=%async_computation | async-start | bytes 3670016 | tf_op jit(solution)/shard_map/all_to_all | solution.py:47
  35.6 87.6 %reduce-scatter.2.cloned.1.call-start = ((), (), s32[]{:S(2)}) async-start(), calls=%async_computation.2 | async-start | bytes 4128768 | tf_op jit(solution)/shard_map/reduce_scatter | solution.py:65
  79.1 87.1 %all-gather.2.cloned.1.call-start = ((), (), s32[]{:S(2)}) async-start(), calls=%async_computation.3 | async-start | bytes 4128768 | tf_op jit(solution)/shard_map/all_gather | solution.py:68
Sparse Core Ops, SparseCore 0:
  79.2 43.9 reduce-scatter.1
  125.2 40.9 all-gather.1
